TPU v7x, 256 devices: a whole 4x4x8 slice. The times are simulated.
256 devices in a mesh: grp: 16 (over z, y_hi), ep: 16 (over y_lo, x, core).
Axes of the slice: x: 4, y: 4 (y_hi: 2, y_lo: 2; y = y_hi * 2 + y_lo), z: 8, core: 2. Of those that a mesh axis runs over, the one named last changes fastest.
Arguments:
- tokens: bfloat16 [49152, 4096], P(('grp', 'ep')), may hold values from -6 to 6
- expert_ids: int32 [49152, 8], P(('grp', 'ep')), may hold values from 0 to 127, all different within a row; in each aligned block of 192 rows (0 to 191, 192 to 383, ...) at most 24 rows name the same one
- gate_probs: float32 [49152, 8], P(('grp', 'ep')), may hold values from 0.02 to 0.25
- placement: int32 [16, 4], P('grp'), may hold values from 0 to 1
- gate_weight: bfloat16 [16, 4096, 3072], P('grp', None, 'ep'), may hold values from -0.09375 to 0.09375
- up_weight: bfloat16 [16, 4096, 3072], P('grp', None, 'ep'), may hold values from -0.09375 to 0.09375
- down_weight: bfloat16 [16, 3072, 4096], P('grp', 'ep'), may hold values from -0.21875 to 0.21875
- out_grad: bfloat16 [49152, 4096], P(('grp', 'ep')), may hold values from -6 to 6
- moment_first: float32 [2, 3072, 4096], P(None, 'ep', 'grp'), may hold values from -2 to 2
- moment_second: float32 [2, 3072, 4096], P(None, 'ep', 'grp'), may hold values from 0.01 to 1
Outputs:
- token_grad: bfloat16 [49152, 4096], P(('grp', 'ep'))
- step_dir: bfloat16 [16, 3072, 4096], P('grp', 'ep')
- new_first: float32 [2, 3072, 4096], P(None, 'ep', 'grp')
- new_second: float32 [2, 3072, 4096], P(None, 'ep', 'grp')
Inputs may be any that keep to these rules, and one draw needn't show every extreme that they name: `expert_ids`: each row names 8 different experts. In the rows of one device no expert is named more than 24 times, a bound that some block reaches. Group g holds expert placement[g, s] * 4 + s in its slot s.
All inputs are finite; a program needn't handle non-finite values.
Results may differ from a plain program's by a relative error of at most 0.015.
Values may be sent and summed in bfloat16 or wider, within the bound.
A program may use at most 128 MiB of HBM per device.

v0:
```python
import math
import jax
import jax.numpy as jnp
from jax import lax
from jax.sharding import PartitionSpec as P

QUARTERS = 4
CANDS = 2
CAP = 24
beta_one = 0.9
beta_two = 0.999
adam_eps = 1e-08
first_fix = 1.0 - math.exp(1000.0 * math.log(0.9))
second_fix = 1.0 - math.exp(1000.0 * math.log(0.999))


def moments(gradient, first_moment, second):
    new_first = beta_one * first_moment + (1.0 - beta_one) * gradient
    new_second = beta_two * second + (1.0 - beta_two) * gradient * gradient
    return (new_first, new_second)


def direction(new_first, new_second):
    return new_first / first_fix / (jnp.sqrt(new_second / second_fix) + adam_eps)


def body(
    tokens,
    expert_ids,
    gate_probs,
    placement,
    gate_weight,
    up_weight,
    down_weight,
    out_grad,
    moment_first,
    moment_second,
):
    num_ep = lax.axis_size("ep")
    slot_count = num_ep // QUARTERS
    tok_count = tokens.shape[0]
    width = tokens.shape[1]
    held_ids = placement[0] * slot_count + jnp.arange(slot_count, dtype=jnp.int32)
    matches = expert_ids[:, :, None] == held_ids[None, None, :]
    hit_rows = jnp.any(matches, axis=1)
    coeffs = jnp.sum(jnp.where(matches, gate_probs[:, :, None], jnp.float32(0.0)), axis=1)
    ranking = jnp.cumsum(hit_rows.astype(jnp.int32), axis=0) - 1
    select_mask = hit_rows.T[:, None, :] & (
        ranking.T[:, None, :] == jnp.arange(CAP, dtype=jnp.int32)[None, :, None]
    )
    select_flat = select_mask.reshape(slot_count * CAP, tok_count).astype(jnp.bfloat16)
    send_tokens = jnp.dot(select_flat, tokens, preferred_element_type=jnp.float32).astype(
        jnp.bfloat16
    )
    send_grads = jnp.dot(select_flat, out_grad, preferred_element_type=jnp.float32).astype(
        jnp.bfloat16
    )
    send_coeffs = jnp.sum(select_mask.astype(jnp.float32) * coeffs.T[:, None, :], axis=2)

    def spread(source):
        shaped = source.reshape(slot_count, 1, CAP, width)
        return jnp.broadcast_to(shaped, (slot_count, QUARTERS, CAP, width)).reshape(
            num_ep, CAP, width
        )

    coeff_spread = jnp.broadcast_to(send_coeffs[:, None, :], (slot_count, QUARTERS, CAP)).reshape(
        num_ep, CAP
    )
    w_gate = gate_weight[0]
    w_up = up_weight[0]
    w_down = down_weight[0]
    recv_tokens, recv_grads, recv_coeffs = (
        lax.all_to_all(spread(send_tokens), "ep", split_axis=0, concat_axis=0, tiled=True),
        lax.all_to_all(spread(send_grads), "ep", split_axis=0, concat_axis=0, tiled=True),
        lax.all_to_all(
            coeff_spread.astype(jnp.bfloat16), "ep", split_axis=0, concat_axis=0, tiled=True
        ).astype(coeff_spread.dtype),
    )
    in_rows = recv_tokens.reshape(num_ep * CAP, width)
    pre_gate = jnp.dot(in_rows, w_gate, preferred_element_type=jnp.float32)
    pre_up = jnp.dot(in_rows, w_up, preferred_element_type=jnp.float32)
    sigmoid_gate = jax.nn.sigmoid(pre_gate)
    activated = pre_gate * sigmoid_gate
    hidden = (activated * pre_up).astype(jnp.bfloat16)
    pre_gate, pre_up, sigmoid_gate, activated, hidden = (
        pre_gate,
        pre_up,
        sigmoid_gate,
        activated,
        hidden,
    )
    scaled = (
        recv_coeffs.reshape(num_ep * CAP)[:, None]
        * recv_grads.reshape(num_ep * CAP, width).astype(jnp.float32)
    ).astype(jnp.bfloat16)
    d_hidden = jnp.einsum("rd,hd->rh", scaled, w_down, preferred_element_type=jnp.float32)
    weight_grad = jnp.einsum("rh,rd->hd", hidden, scaled, preferred_element_type=jnp.float32)
    d_gate = (d_hidden * pre_up * sigmoid_gate * (1.0 + pre_gate * (1.0 - sigmoid_gate))).astype(
        jnp.bfloat16
    )
    d_up = (d_hidden * activated).astype(jnp.bfloat16)
    partial_value = jnp.einsum("rh,dh->rd", d_gate, w_gate, preferred_element_type=jnp.float32)
    partial_value = (
        partial_value + jnp.einsum("rh,dh->rd", d_up, w_up, preferred_element_type=jnp.float32)
    ).astype(jnp.bfloat16)
    returned = lax.all_to_all(
        partial_value.reshape(num_ep, CAP, width), "ep", split_axis=0, concat_axis=0, tiled=True
    )
    combine = jnp.broadcast_to(
        select_mask.reshape(slot_count, 1, CAP, tok_count), (slot_count, QUARTERS, CAP, tok_count)
    )
    combine = combine.reshape(num_ep * CAP, tok_count).astype(jnp.bfloat16)
    token_grad = jnp.einsum(
        "kt,kd->td",
        combine,
        returned.reshape(num_ep * CAP, width),
        preferred_element_type=jnp.float32,
    ).astype(jnp.bfloat16)
    ep_index = lax.axis_index("ep")
    my_cand = lax.dynamic_index_in_dim(placement[0], ep_index // QUARTERS, 0, keepdims=False)
    cand_mask = (jnp.arange(CANDS, dtype=jnp.int32) == my_cand).astype(jnp.float32)
    cand_grads = cand_mask[:, None, None] * weight_grad[None]
    totals = lax.psum(cand_grads.astype(jnp.bfloat16), "grp").astype(jnp.float32)
    full_first, full_second = (
        lax.all_gather(moment_first.astype(jnp.bfloat16), "grp", axis=2, tiled=True).astype(
            moment_first.dtype
        ),
        lax.all_gather(moment_second.astype(jnp.bfloat16), "grp", axis=2, tiled=True).astype(
            moment_second.dtype
        ),
    )
    share_cols = moment_first.shape[2]
    share_start = lax.axis_index("grp") * share_cols
    new_first, new_second = moments(
        lax.dynamic_slice_in_dim(totals, share_start, share_cols, 2), moment_first, moment_second
    )
    own_grad = lax.dynamic_index_in_dim(totals, my_cand, 0, keepdims=True)
    own_first = lax.dynamic_index_in_dim(full_first, my_cand, 0, keepdims=True)
    own_second = lax.dynamic_index_in_dim(full_second, my_cand, 0, keepdims=True)
    copy_first, copy_second = moments(own_grad, own_first, own_second)
    step_dir = direction(copy_first, copy_second).astype(jnp.bfloat16)
    return (token_grad, step_dir, new_first, new_second)


def solution(mesh):
    return jax.shard_map(
        body,
        mesh=mesh,
        in_specs=(
            P(("grp", "ep"), None),
            P(("grp", "ep"), None),
            P(("grp", "ep"), None),
            P("grp", None),
            P("grp", None, "ep"),
            P("grp", None, "ep"),
            P("grp", "ep", None),
            P(("grp", "ep"), None),
            P(None, "ep", "grp"),
            P(None, "ep", "grp"),
        ),
        out_specs=(
            P(("grp", "ep"), None),
            P("grp", "ep", None),
            P(None, "ep", "grp"),
            P(None, "ep", "grp"),
        ),
        check_vma=False,
    )
```

profile of v0, /device:TPU:2, one launch (start us, length us, event | category | flops | bytes accessed | tf_op | source)
XLA Modules:
  0.0 527.4 jit_solution(9174069582011565920)
XLA Ops:
  11.9 5.9 %all-to-all-start = ((bf16[16,1,24]{2,1,0:T(2,128)(2,1)}), bf16[16,1,24]{2,1,0:T(2,128)(2,1)S(1)}, u32[]{:S(2)}, u32[]{:S(2)}) async-start(bf16[16,1,24]{2,1,0:T(2,128)(2,1)} %copy.29), calls=%async_computation | async-start | bytes 16384 | tf_op jit(solution)/shard_map/all_to_all | solution.py:75
  18.0 1.8 convolution_convert_fusion.1
  19.8 2.6 all-to-all-done
  22.4 2.1 broadcast_in_dim.53
  24.5 5.7 %all-to-all-start.2 = ((bf16[16,24,4096]{2,1,0:T(8,128)(2,1)}), bf16[16,24,4096]{2,1,0:T(8,128)(2,1)}, u32[]{:S(2)}, u32[]{:S(2)}) async-start(bf16[16,24,4096]{2,1,0:T(8,128)(2,1)} %bitcast.62), calls=%async_computation.2 | async-start | bytes 6291456 | tf_op jit(solution)/shard_map/all_to_all | solution.py:73
  31.9 41.2 %all-to-all-done.2 = bf16[16,24,4096]{2,1,0:T(8,128)(2,1)} async-done(((bf16[16,24,4096]{2,1,0:T(8,128)(2,1)}), bf16[16,24,4096]{2,1,0:T(8,128)(2,1)}, u32[]{:S(2)}, u32[]{:S(2)}) %all-to-all-start.2) | async-done | bytes 3145760 | tf_op jit(solution)/shard_map/all_to_all | solution.py:73
  73.1 2.1 broadcast_in_dim.29
  75.2 4.5 all-to-all-start.1
  81.1 3.1 fusion.9
  84.2 3.8 fusion.12
  88.0 34.3 %all-to-all-done.1 = bf16[16,24,4096]{2,1,0:T(8,128)(2,1)} async-done(((bf16[16,24,4096]{2,1,0:T(8,128)(2,1)}), bf16[16,24,4096]{2,1,0:T(8,128)(2,1)}, u32[]{:S(2)}, u32[]{:S(2)}) %all-to-all-start.1) | async-done | bytes 3145760 | tf_op jit(solution)/shard_map/all_to_all | solution.py:74
  122.3 2.9 fusion
  126.3 2.3 multiply_convert_fusion
  128.6 181.3 %all-reduce.3.cloned.1.call-done = bf16[2,192,4096]{2,1,0:T(8,128)(2,1)} async-done(((bf16[2,192,4096]{2,1,0:T(8,128)(2,1)}), bf16[2,192,4096]{2,1,0:T(8,128)(2,1)}) %all-reduce.3.cloned.1.call-update) | async-done | bytes 3145744 | tf_op jit(solution)/shard_map/psum | solution.py:123
  309.9 2.7 convert_element_type.124
  312.7 2.7 copy-done.1
  317.2 3.0 multiply_convert_fusion.1
  322.5 2.7 add_convert_fusion
  325.3 4.6 all-to-all-start.3
  331.8 40.9 %all-to-all-done.3 = bf16[16,24,4096]{2,1,0:T(8,128)(2,1)} async-done(((bf16[16,24,4096]{2,1,0:T(8,128)(2,1)}), bf16[16,24,4096]{2,1,0:T(8,128)(2,1)}, u32[]{:S(2)}, u32[]{:S(2)}) %all-to-all-start.3) | async-done | bytes 3145760 | tf_op jit(solution)/shard_map/all_to_all | solution.py:106
  372.8 4.1 convolution_convert_fusion
  376.8 43.8 %all-gather.3.cloned.1.call-done = bf16[2,192,4096]{2,1,0:T(8,128)(2,1)} async-done(((bf16[2,192,256]{2,1,0:T(8,128)(2,1)}), bf16[2,192,4096]{2,1,0:T(8,128)(2,1)}) %all-gather.3.cloned.1.call-update) | async-done | bytes 3145744 | tf_op jit(solution)/shard_map/all_gather | solution.py:125
  420.7 94.2 %all-gather.5.cloned.1.call-done = bf16[2,192,4096]{2,1,0:T(8,128)(2,1)} async-done(((bf16[2,192,256]{2,1,0:T(8,128)(2,1)}), bf16[2,192,4096]{2,1,0:T(8,128)(2,1)}) %all-gather.5.cloned.1.call-update) | async-done | bytes 3145744 | tf_op jit(solution)/shard_map/all_gather | solution.py:128
  514.8 6.1 %fusion.6 = bf16[1,192,4096]{2,1,0:T(8,128)(2,1)} fusion(f32[2,192,4096]{2,1,0:T(8,128)} %copy-done.1, s32[]{:T(128)S(6)} %select_n.25, bf16[2,192,4096]{2,1,0:T(8,128)(2,1)} %all-gather.5.cloned.1.call-done, bf16[2,192,4096]{2,1,0:T(8,128)(2,1)} %all-gather.3.cloned.1.call-done), kind=kLoop, calls=%fused_computation.14 | loop fusion | flops 10223616 | bytes 7864324 | tf_op jit(solution)/shard_map/convert_element_type | solution.py:141
  (55 shorter events, 13.3 us)
Async XLA Ops:
  7.2 74.0 %copy-start = (bf16[1,4096,192]{1,2,0:T(8,128)(2,1)S(1)}, bf16[1,4096,192]{1,2,0:T(8,128)(2,1)}, u32[]{:S(2)}) copy-start(bf16[1,4096,192]{1,2,0:T(8,128)(2,1)} %param.14) | copy-start | bytes 4718596
  11.9 10.5 %all-to-all-start = ((bf16[16,1,24]{2,1,0:T(2,128)(2,1)}), bf16[16,1,24]{2,1,0:T(2,128)(2,1)S(1)}, u32[]{:S(2)}, u32[]{:S(2)}) async-start(bf16[16,1,24]{2,1,0:T(2,128)(2,1)} %copy.29), calls=%async_computation | async-start | bytes 16384 | tf_op jit(solution)/shard_map/all_to_all | solution.py:75
  24.5 48.6 %all-to-all-start.2 = ((bf16[16,24,4096]{2,1,0:T(8,128)(2,1)}), bf16[16,24,4096]{2,1,0:T(8,128)(2,1)}, u32[]{:S(2)}, u32[]{:S(2)}) async-start(bf16[16,24,4096]{2,1,0:T(8,128)(2,1)} %bitcast.62), calls=%async_computation.2 | async-start | bytes 6291456 | tf_op jit(solution)/shard_map/all_to_all | solution.py:73
  75.1 4.6 copy-start.8
  75.2 47.2 %all-to-all-start.1 = ((bf16[16,24,4096]{2,1,0:T(8,128)(2,1)}), bf16[16,24,4096]{2,1,0:T(8,128)(2,1)}, u32[]{:S(2)}, u32[]{:S(2)}) async-start(bf16[16,24,4096]{2,1,0:T(8,128)(2,1)} %bitcast.60), calls=%async_computation.1 | async-start | bytes 6291456 | tf_op jit(solution)/shard_map/all_to_all | solution.py:74
  79.7 4.5 copy-start.2
  79.7 230.2 %all-reduce.3.cloned.1.call-start = ((), (), s32[]{:S(2)}) async-start(), calls=%async_computation.5 | async-start | bytes 6291456 | tf_op jit(solution)/shard_map/psum | solution.py:123
  122.3 2.9 copy-start.3
  128.5 292.1 %all-gather.3.cloned.1.call-start = ((), (), s32[]{:S(2)}) async-start(), calls=%async_computation.4 | async-start | bytes 3342336 | tf_op jit(solution)/shard_map/all_gather | solution.py:125
  309.9 5.4 %copy-start.5 = (f32[2,192,256]{2,1,0:T(8,128)S(1)}, f32[2,192,256]{2,1,0:T(8,128)}, u32[]{:S(2)}) copy-start(f32[2,192,256]{2,1,0:T(8,128)} %param.19) | copy-start | bytes 1179652
  309.9 5.4 %copy-start.6 = (f32[2,192,256]{2,1,0:T(8,128)S(1)}, f32[2,192,256]{2,1,0:T(8,128)}, u32[]{:S(2)}) copy-start(f32[2,192,256]{2,1,0:T(8,128)} %param.18) | copy-start | bytes 1179652
  312.7 2.7 copy-start.1
  316.4 198.4 %all-gather.5.cloned.1.call-start = ((), (), s32[]{:S(2)}) async-start(), calls=%async_computation.6 | async-start | bytes 3342336 | tf_op jit(solution)/shard_map/all_gather | solution.py:128
  317.2 3.0 copy-start.7
  320.2 1.2 copy-start.4
  325.3 47.5 %all-to-all-start.3 = ((bf16[16,24,4096]{2,1,0:T(8,128)(2,1)}), bf16[16,24,4096]{2,1,0:T(8,128)(2,1)}, u32[]{:S(2)}, u32[]{:S(2)}) async-start(bf16[16,24,4096]{2,1,0:T(8,128)(2,1)} %bitcast.61), calls=%async_computation.3 | async-start | bytes 6291456 | tf_op jit(solution)/shard_map/all_to_all | solution.py:106
Sparse Core Ops, SparseCore 0:
  128.7 181.2 all-reduce.2
  316.6 104.0 all-gather.2
  423.1 91.6 all-gather.4
where the time goes:
time: 528 us; the launch traced here: 527 us
  waiting for transfers between devices  439 us (83%)
  other arithmetic  22.7 us (4%)
  starting transfers between devices  20.7 us (4%)
  matrix products  20.5 us (4%)
  between operations  16 us (3%)
  local copies, waits for them, and re-layouts  8.52 us (2%)
    psum x1, waiting for transfers between devices, body(): lax.psum(cand_grads.astype(jnp.bfloat16), 'grp').astype(jnp.float32)  181 us
    all_gather x1, waiting for transfers between devices, body(): lax.all_gather(moment_second.astype(jnp.bfloat16), 'grp', axis=2, tiled=T...  94.2 us
    all_gather x1, waiting for transfers between devices, body(): lax.all_gather(moment_first.astype(jnp.bfloat16), 'grp', axis=2, tiled=True)  43.8 us
    all_to_all x1, waiting for transfers between devices, body(): lax.all_to_all(spread(send_tokens), 'ep', split_axis=0, concat_axis=0, ti...  41.2 us
    all_to_all x1, waiting for transfers between devices, body(): lax.all_to_all(partial_value.reshape(num_ep, CAP, width), 'ep', split_axi...  40.9 us
    all_to_all x1, waiting for transfers between devices, body(): lax.all_to_all(spread(send_grads), 'ep', split_axis=0, concat_axis=0, til...  34.3 us
  transfers between devices with their start and end apart: 7, of which 7 were waited for; matrix products, arithmetic and copies ran while one was open for 5% of the time, Pallas kernels for 0%

commit v1 on v0

--- a/solution.py
+++ b/solution.py
@@ -122,9 +122,12 @@
     cand_grads = cand_mask[:, None, None] * weight_grad[None]
     totals = lax.psum(cand_grads.astype(jnp.bfloat16), "grp").astype(jnp.float32)
     full_first, full_second = (
-        lax.all_gather(moment_first.astype(jnp.bfloat16), "grp", axis=2, tiled=True).astype(
-            moment_first.dtype
-        ),
+        jnp.concatenate(
+            lax.all_to_all(
+                jnp.stack([moment_first.astype(jnp.bfloat16)] * lax.axis_size("grp")), "grp", 0, 0
+            ),
+            axis=2,
+        ).astype(moment_first.dtype),
         lax.all_gather(moment_second.astype(jnp.bfloat16), "grp", axis=2, tiled=True).astype(
             moment_second.dtype
         ),

time: 528 us -> 502 us (0.951)
  waiting for transfers between devices: 439 us -> 393 us
  local copies, waits for them, and re-layouts: 8.52 us -> 15.7 us
  matrix products: 20.5 us -> 25.9 us
    all_to_all x0 -> x1, waiting for transfers between devices: none -> 65.9 us  [body(): lax.all_to_all(jnp.stack([moment_first.astype(jnp.bfloat16)] * lax.axis_s...]
    all_gather x1, waiting for transfers between devices: 94.2 us -> 47.7 us  [body(): lax.all_gather(moment_second.astype(jnp.bfloat16), 'grp', axis=2, tiled=T...]
    all_gather x1 -> x0, waiting for transfers between devices: 43.8 us -> none  [body(): lax.all_gather(moment_first.astype(jnp.bfloat16), 'grp', axis=2, tiled=True)]
    all_to_all x1, waiting for transfers between devices: 40.9 us -> 0.01 us  [body(): lax.all_to_all(partial_value.reshape(num_ep, CAP, width), 'ep', split_axi...]
    psum x1, waiting for transfers between devices: 181 us -> 200 us  [body(): lax.psum(cand_grads.astype(jnp.bfloat16), 'grp').astype(jnp.float32)]
  transfers between devices with their start and end apart: 7 -> 7, of which waited for: 7 -> 6; matrix products, arithmetic and copies ran while one was open for 5% -> 6% of each run, Pallas kernels for 0% -> 0%
where the time goes in v1:
time: 502 us
  waiting for transfers between devices  393 us (78%)
  matrix products  25.9 us (5%)
  other arithmetic  25.6 us (5%)
  starting transfers between devices  25.6 us (5%)
  between operations  16.3 us (3%)
  local copies, waits for them, and re-layouts  15.7 us (3%)
    psum x1, waiting for transfers between devices, body(): lax.psum(cand_grads.astype(jnp.bfloat16), 'grp').astype(jnp.float32)  200 us
    all_to_all x1, waiting for transfers between devices, body(): lax.all_to_all(jnp.stack([moment_first.astype(jnp.bfloat16)] * lax.axis_s...  65.9 us
    all_gather x1, waiting for transfers between devices, body(): lax.all_gather(moment_second.astype(jnp.bfloat16), 'grp', axis=2, tiled=T...  47.7 us
    all_to_all x1, waiting for transfers between devices, body(): lax.all_to_all(spread(send_tokens), 'ep', split_axis=0, concat_axis=0, ti...  41.1 us
    all_to_all x1, waiting for transfers between devices, body(): lax.all_to_all(spread(send_grads), 'ep', split_axis=0, concat_axis=0, til...  34.3 us
  transfers between devices with their start and end apart: 7, of which 6 were waited for; matrix products, arithmetic and copies ran while one was open for 6% of the time, Pallas kernels for 0%

profile of v1, /device:TPU:2, one launch (start us, length us, event | category | flops | bytes accessed | tf_op | source)
XLA Modules:
  0.0 501.6 jit_solution(17101681857297368069)
XLA Ops:
  11.9 5.9 %all-to-all-start = ((bf16[16,1,24]{2,1,0:T(2,128)(2,1)}), bf16[16,1,24]{2,1,0:T(2,128)(2,1)S(1)}, u32[]{:S(2)}, u32[]{:S(2)}) async-start(bf16[16,1,24]{2,1,0:T(2,128)(2,1)} %copy.30), calls=%async_computation | async-start | bytes 16384 | tf_op jit(solution)/shard_map/all_to_all | solution.py:75
  19.8 2.6 all-to-all-done
  24.5 5.7 %all-to-all-start.2 = ((bf16[16,24,4096]{2,1,0:T(8,128)(2,1)}), bf16[16,24,4096]{2,1,0:T(8,128)(2,1)}, u32[]{:S(2)}, u32[]{:S(2)}) async-start(bf16[16,24,4096]{2,1,0:T(8,128)(2,1)} %bitcast.67), calls=%async_computation.2 | async-start | bytes 6291456 | tf_op jit(solution)/shard_map/all_to_all | solution.py:73
  31.9 41.1 %all-to-all-done.2 = bf16[16,24,4096]{2,1,0:T(8,128)(2,1)} async-done(((bf16[16,24,4096]{2,1,0:T(8,128)(2,1)}), bf16[16,24,4096]{2,1,0:T(8,128)(2,1)}, u32[]{:S(2)}, u32[]{:S(2)}) %all-to-all-start.2) | async-done | bytes 3145760 | tf_op jit(solution)/shard_map/all_to_all | solution.py:73
  75.1 4.5 all-to-all-start.1
  81.1 3.1 fusion.9
  84.2 3.8 fusion.12
  88.0 34.3 %all-to-all-done.1 = bf16[16,24,4096]{2,1,0:T(8,128)(2,1)} async-done(((bf16[16,24,4096]{2,1,0:T(8,128)(2,1)}), bf16[16,24,4096]{2,1,0:T(8,128)(2,1)}, u32[]{:S(2)}, u32[]{:S(2)}) %all-to-all-start.1) | async-done | bytes 3145760 | tf_op jit(solution)/shard_map/all_to_all | solution.py:74
  122.3 3.0 multiply_convert_fusion.1
  127.2 3.7 fusion.7
  131.0 2.9 fusion
  134.9 2.3 multiply_convert_fusion
  138.1 5.5 %add_convert_fusion = bf16[384,4096]{1,0:T(8,128)(2,1)} fusion(f32[384,4096]{1,0:T(8,128)} %fusion.7, bf16[1,4096,192]{1,2,0:T(8,128)(2,1)S(1)} %copy-done.3, f32[384,192]{0,1:T(8,128)S(1)} %copy-done.5, f32[384,192]{0,1:T(8,128)S(1)} %fusion.9), kind=kOutput, calls=%fused_computation.4 | convolution fusion | flops 607567872 | bytes 11599872 | tf_op jit(solution)/shard_map/rh,dh->rd/dot_general | solution.py:104
  143.6 4.4 all-to-all-start.3
  148.0 200.4 %all-reduce.3.cloned.1.call-done = bf16[2,192,4096]{2,1,0:T(8,128)(2,1)} async-done(((bf16[2,192,4096]{2,1,0:T(8,128)(2,1)}), bf16[2,192,4096]{2,1,0:T(8,128)(2,1)}) %all-reduce.3.cloned.1.call-update) | async-done | bytes 3145744 | tf_op jit(solution)/shard_map/psum | solution.py:123
  348.3 2.6 convert_element_type.132
  351.0 2.7 copy-done.2
  356.7 4.9 all-to-all-start.4
  364.3 4.1 convolution_convert_fusion
  368.4 65.9 %all-to-all-done.4 = bf16[16,2,192,256]{3,2,1,0:T(8,128)(2,1)} async-done(((bf16[16,2,192,256]{3,2,1,0:T(8,128)(2,1)}), bf16[16,2,192,256]{3,2,1,0:T(8,128)(2,1)}, u32[]{:S(2)}, u32[]{:S(2)}) %all-to-all-start.4) | async-done | bytes 3145760 | tf_op jit(solution)/shard_map/all_to_all | solution.py:126
  434.3 2.7 convert_bitcast_fusion
  437.0 3.5 copy.32
  440.5 47.7 %all-gather.2.cloned.1.call-done = bf16[2,192,4096]{2,1,0:T(8,128)(2,1)} async-done(((bf16[2,192,256]{2,1,0:T(8,128)(2,1)}), bf16[2,192,4096]{2,1,0:T(8,128)(2,1)}) %all-gather.2.cloned.1.call-update) | async-done | bytes 3145744 | tf_op jit(solution)/shard_map/all_gather | solution.py:131
  488.2 6.5 %fusion.6 = bf16[1,192,4096]{2,1,0:T(8,128)(2,1)} fusion(f32[2,192,4096]{2,1,0:T(8,128)} %copy-done.2, s32[]{:T(128)S(6)} %select_n.25, f32[2,192,4096]{2,1,0:T(8,128)} %bitcast.64, bf16[2,192,4096]{2,1,0:T(8,128)(2,1)} %all-gather.2.cloned.1.call-done), kind=kLoop, calls=%fused_computation.15 | loop fusion | flops 9437184 | bytes 9437188 | tf_op jit(solution)/shard_map/convert_element_type | solution.py:144
  (61 shorter events, 21.7 us)
Async XLA Ops:
  7.2 74.0 %copy-start = (bf16[1,4096,192]{1,2,0:T(8,128)(2,1)S(1)}, bf16[1,4096,192]{1,2,0:T(8,128)(2,1)}, u32[]{:S(2)}) copy-start(bf16[1,4096,192]{1,2,0:T(8,128)(2,1)} %param.14) | copy-start | bytes 4718596
  11.9 10.5 %all-to-all-start = ((bf16[16,1,24]{2,1,0:T(2,128)(2,1)}), bf16[16,1,24]{2,1,0:T(2,128)(2,1)S(1)}, u32[]{:S(2)}, u32[]{:S(2)}) async-start(bf16[16,1,24]{2,1,0:T(2,128)(2,1)} %copy.30), calls=%async_computation | async-start | bytes 16384 | tf_op jit(solution)/shard_map/all_to_all | solution.py:75
  24.5 48.6 %all-to-all-start.2 = ((bf16[16,24,4096]{2,1,0:T(8,128)(2,1)}), bf16[16,24,4096]{2,1,0:T(8,128)(2,1)}, u32[]{:S(2)}, u32[]{:S(2)}) async-start(bf16[16,24,4096]{2,1,0:T(8,128)(2,1)} %bitcast.67), calls=%async_computation.2 | async-start | bytes 6291456 | tf_op jit(solution)/shard_map/all_to_all | solution.py:73
  75.1 4.6 copy-start.10
  75.1 47.2 %all-to-all-start.1 = ((bf16[16,24,4096]{2,1,0:T(8,128)(2,1)}), bf16[16,24,4096]{2,1,0:T(8,128)(2,1)}, u32[]{:S(2)}, u32[]{:S(2)}) async-start(bf16[16,24,4096]{2,1,0:T(8,128)(2,1)} %bitcast.65), calls=%async_computation.1 | async-start | bytes 6291456 | tf_op jit(solution)/shard_map/all_to_all | solution.py:74
  79.7 4.6 copy-start.3
  79.7 268.7 %all-reduce.3.cloned.1.call-start = ((), (), s32[]{:S(2)}) async-start(), calls=%async_computation.5 | async-start | bytes 6291456 | tf_op jit(solution)/shard_map/psum | solution.py:123
  122.3 3.0 copy-start.9
  125.3 1.9 copy-start.6
  126.5 0.7 copy-start.4
  137.1 1.0 copy-start.5
  143.6 211.1 %all-to-all-start.3 = ((bf16[16,24,4096]{2,1,0:T(8,128)(2,1)}), bf16[16,24,4096]{2,1,0:T(8,128)(2,1)}, u32[]{:S(2)}, u32[]{:S(2)}) async-start(bf16[16,24,4096]{2,1,0:T(8,128)(2,1)} %bitcast.66), calls=%async_computation.3 | async-start | bytes 6291456 | tf_op jit(solution)/shard_map/all_to_all | solution.py:106
  148.0 205.7 %copy-start.7 = (f32[2,192,256]{2,1,0:T(8,128)S(1)}, f32[2,192,256]{2,1,0:T(8,128)}, u32[]{:S(2)}) copy-start(f32[2,192,256]{2,1,0:T(8,128)} %param.19) | copy-start | bytes 1179652
  148.0 205.7 %copy-start.8 = (f32[2,192,256]{2,1,0:T(8,128)S(1)}, f32[2,192,256]{2,1,0:T(8,128)}, u32[]{:S(2)}) copy-start(f32[2,192,256]{2,1,0:T(8,128)} %param.18) | copy-start | bytes 1179652
  351.0 2.7 copy-start.2
  356.7 77.6 %all-to-all-start.4 = ((bf16[16,2,192,256]{3,2,1,0:T(8,128)(2,1)}), bf16[16,2,192,256]{3,2,1,0:T(8,128)(2,1)}, u32[]{:S(2)}, u32[]{:S(2)}) async-start(bf16[16,2,192,256]{3,2,1,0:T(8,128)(2,1)} %stack.2), calls=%async_computation.4 | async-start | bytes 6291456 | tf_op jit(solution)/shard_map/all_to_all | solution.py:126
  361.6 126.6 %all-gather.2.cloned.1.call-start = ((), (), s32[]{:S(2)}) async-start(), calls=%async_computation.6 | async-start | bytes 3342336 | tf_op jit(solution)/shard_map/all_gather | solution.py:131
  488.2 6.5 %copy-start.1 = (bf16[1,4096,192]{1,2,0:T(8,128)(2,1)S(1)}, bf16[1,4096,192]{1,2,0:T(8,128)(2,1)}, u32[]{:S(2)}) copy-start(bf16[1,4096,192]{1,2,0:T(8,128)(2,1)} %param.14) | copy-start | bytes 4718596
Sparse Core Ops, SparseCore 0:
  137.3 211.0 all-reduce.2
  365.5 122.7 all-gather.1
